TPU v7x, 32 devices: a whole 2x2x4 slice. The times are simulated.
32 devices in a mesh: groups: 2 (over y), leaf: 4 (over z), rows: 2 (over x), rhs: 2 (over core).
Axes of the slice: x: 2, y: 2, z: 4, core: 2. Of those that a mesh axis runs over, the one named last changes fastest.
Arguments:
- rhs: float32 [7168, 768], P(('groups', 'leaf', 'rows'), 'rhs'), parts along dimension 0, may hold values from -6 to 6
- dinv: float32 [7168, 512], P(('groups', 'leaf'), 'rows'), parts along dimension 0, may hold values from -3 to 3
- lower: float32 [10240, 512], P(('groups', 'leaf'), 'rows'), parts along dimension 0, may hold values from -0.25 to 0.25
- pattern: int32 [8, 3], P(('groups', 'leaf')), parts along dimension 0, may hold values 0 or 1
Outputs:
- solution: float32 [7168, 768], P(('groups', 'leaf', 'rows'), 'rhs'), parts along dimension 0
There are 2 independent parts, one for each index of `groups`. A program takes and returns all parts, laid end to end along the dimension named above; each array names one. Nothing has to cross between parts.
All inputs are finite; a program needn't handle non-finite values. No bound on the sum of `pattern` on one device may be relied on, other than what follows from the above.
Results may differ from a plain program's by a relative error of at most 0.00015.
Values sent between devices are 32-bit elements; how exact they have to be, the bound alone decides.
A program may use at most 64 MiB of HBM per device.

v0:
```python
import jax
import jax.numpy as jnp
from jax import lax
from jax.sharding import PartitionSpec as P

S = 512


def partner(value, axis, distance):
    mask = 2**distance
    pairs = [(source, source ^ mask) for source in range(lax.axis_size(axis))]
    return lax.ppermute(value, axis, pairs)


def subtree_total(summand, tree_depth):
    for bit_index in range(tree_depth):
        summand = summand + partner(summand, "leaf", bit_index)
    return summand


def contract_rows(matrix, vectors):
    return lax.dot_general(
        matrix,
        vectors,
        (((0,), (0,)), ((), ())),
        precision=lax.Precision.HIGHEST,
        preferred_element_type=jnp.float32,
    )


def body(rhs, dinv, lower, pattern):
    highest = lax.Precision.HIGHEST
    levels = lax.axis_size("leaf").bit_length() - 1
    row_split = lax.axis_size("rows")
    leaf_index = lax.axis_index("leaf")
    row_block = dinv.shape[1]
    rhs_cols = rhs.shape[1]
    block_masks = pattern[0].astype(jnp.float32)
    widths = [S >> tree_level for tree_level in range(levels + 1)]
    inverse_offsets = []
    offset = 0
    for node_width in widths:
        inverse_offsets.append(offset)
        offset += node_width
    sections = {}
    lower_offset = 0
    section = 0
    for tree_level in range(levels):
        for upper_level in range(tree_level + 1, levels + 1):
            sections[tree_level, upper_level] = (lower_offset, section)
            lower_offset += widths[tree_level]
            section += 1
    pending = [jnp.zeros((row_block, rhs_cols), jnp.float32) for tree_level in range(levels + 1)]
    solved = []
    for tree_level in range(levels + 1):
        node_width = widths[tree_level]
        row_share = node_width // row_split
        rhs_offset = inverse_offsets[tree_level] // row_split
        first_row = leaf_index % (1 << tree_level) * row_share
        own_rows = rhs[rhs_offset : rhs_offset + row_share]
        padded = lax.dynamic_update_slice_in_dim(
            jnp.zeros((row_block, rhs_cols), jnp.float32), own_rows, first_row, 0
        )
        reduced = subtree_total(padded - pending[tree_level], tree_level)
        inverse_block = dinv[inverse_offsets[tree_level] : inverse_offsets[tree_level] + node_width]
        local_product = jnp.dot(
            inverse_block, reduced, precision=highest, preferred_element_type=jnp.float32
        )
        solved_part = lax.psum(local_product, "rows")
        solved.append(solved_part)
        for upper_level in range(tree_level + 1, levels + 1):
            start_row, index_pair = sections[tree_level, upper_level]
            coupling = lower[start_row : start_row + node_width]
            pending[upper_level] = pending[upper_level] + block_masks[index_pair] * contract_rows(
                coupling, solved_part
            )
    answers = [None] * (levels + 1)
    for tree_level in reversed(range(levels + 1)):
        node_width = widths[tree_level]
        remainder = solved[tree_level]
        if tree_level < levels:
            partial_value = jnp.zeros((node_width, rhs_cols), jnp.float32)
            for upper_level in range(tree_level + 1, levels + 1):
                start_row, index_pair = sections[tree_level, upper_level]
                coupling = lower[start_row : start_row + node_width]
                partial_value = partial_value + block_masks[index_pair] * jnp.dot(
                    coupling,
                    answers[upper_level],
                    precision=highest,
                    preferred_element_type=jnp.float32,
                )
            remainder = remainder - lax.psum(partial_value, "rows")
        inverse_block = dinv[inverse_offsets[tree_level] : inverse_offsets[tree_level] + node_width]
        answers[tree_level] = subtree_total(contract_rows(inverse_block, remainder), tree_level)
    pieces = []
    for tree_level in range(levels + 1):
        row_share = widths[tree_level] // row_split
        first_row = leaf_index % (1 << tree_level) * row_share
        pieces.append(lax.dynamic_slice_in_dim(answers[tree_level], first_row, row_share, 0))
    return jnp.concatenate(pieces, axis=0)


def solution(mesh):
    placed = (
        P(("groups", "leaf", "rows"), "rhs"),
        P(("groups", "leaf"), "rows"),
        P(("groups", "leaf"), "rows"),
        P(("groups", "leaf"), None),
    )
    return jax.shard_map(
        body,
        mesh=mesh,
        in_specs=placed,
        out_specs=P(("groups", "leaf", "rows"), "rhs"),
        check_vma=False,
    )
```

profile of v0, /device:TPU:0, one launch (start us, length us, event | category | flops | bytes accessed | tf_op | source)
XLA Modules:
  0.0 265.6 jit_solution(812098645189812947)
XLA Ops:
  6.5 3.1 %fusion.14 = f32[512,384]{1,0:T(8,128)} fusion(f32[896,256]{1,0:T(8,128)} %param.5, f32[448,384]{1,0:T(8,128)} %param.4), kind=kOutput, calls=%fused_computation.26 | convolution fusion | flops 603979776 | bytes 1703936 | tf_op jit(solution)/shard_map/dot_general | solution.py:66
  9.7 0.0 all-reduce.6.cloned.1.call-update
  9.7 0.0 all-reduce.8.cloned.1.call-start
  9.8 0.1 copy.7
  9.9 0.7 fusion.26
  10.7 36.2 %all-reduce.6.cloned.1.call-done = f32[512,384]{1,0:T(8,128)} async-done(((f32[512,384]{1,0:T(8,128)}), f32[512,384]{1,0:T(8,128)}) %all-reduce.6.cloned.1.call-update) | async-done | bytes 786448 | tf_op jit(solution)/shard_map/psum | solution.py:69
  46.9 3.2 %fusion.3 = f32[256,384]{0,1:T(8,128)S(1)} fusion(f32[256,384]{0,1:T(8,128)S(1)} %constant_dynamic-update-slice_fusion, f32[512,384]{1,0:T(8,128)} %all-reduce.6.cloned.1.call-done, f32[1280,256]{1,0:T(8,128)S(1)} %copy-done.1, f32[]{:T(128)} %bitcast), kind=kOutput, calls=%fused_computation.11 | convolution fusion | flops 604176384 | bytes 2097156 | tf_op jit(solution)/shard_map/dot_general | solution.py:22
  50.1 0.0 slice-start.1
  50.1 1.6 collective-permute-start
  51.7 9.4 %collective-permute-done = f32[256,384]{0,1:T(8,128)S(1)} collective-permute-done((f32[256,384]{0,1:T(8,128)S(1)}, f32[256,384]{0,1:T(8,128)S(1)}, u32[]{:S(2)}, u32[]{:S(2)}) %collective-permute-start) | collective-permute-done | bytes 393248 | tf_op jit(solution)/shard_map/ppermute | solution.py:12
  61.1 1.3 convolution_bitcast_fusion.3
  62.3 0.0 all-reduce.8.cloned.1.call-update
  62.4 0.0 all-reduce.10.cloned.1.call-start
  62.4 0.8 copy.8
  63.3 2.0 dynamic_update_slice.8
  65.3 22.9 %all-reduce.8.cloned.1.call-done = f32[256,384]{0,1:T(8,128)} async-done(((f32[256,384]{0,1:T(8,128)}), f32[256,384]{0,1:T(8,128)}) %all-reduce.8.cloned.1.call-update) | async-done | bytes 393232 | tf_op jit(solution)/shard_map/psum | solution.py:69
  88.2 2.1 convolution_multiply_fusion.5
  90.4 2.1 fusion.6
  92.4 1.6 collective-permute-start.1
  94.0 9.4 %collective-permute-done.1 = f32[256,384]{0,1:T(8,128)S(1)} collective-permute-done((f32[256,384]{0,1:T(8,128)S(1)}, f32[256,384]{0,1:T(8,128)S(1)}, u32[]{:S(2)}, u32[]{:S(2)}) %collective-permute-start.1) | collective-permute-done | bytes 393248 | tf_op jit(solution)/shard_map/ppermute | solution.py:12
  103.4 0.1 add.68
  103.4 2.5 collective-permute-start.2
  105.9 16.9 %collective-permute-done.2 = f32[256,384]{0,1:T(8,128)S(1)} collective-permute-done((f32[256,384]{0,1:T(8,128)S(1)}, f32[256,384]{0,1:T(8,128)S(1)}, u32[]{:S(2)}, u32[]{:S(2)}) %collective-permute-start.2) | collective-permute-done | bytes 393248 | tf_op jit(solution)/shard_map/ppermute | solution.py:12
  122.8 1.2 convolution_bitcast_fusion.4
  123.9 0.0 all-reduce.10.cloned.1.call-update
  124.0 0.0 all-reduce.12.cloned.1.call-start
  124.0 22.4 %all-reduce.10.cloned.1.call-done = f32[128,384]{0,1:T(8,128)} async-done(((f32[128,384]{0,1:T(8,128)}), f32[128,384]{0,1:T(8,128)}) %all-reduce.10.cloned.1.call-update) | async-done | bytes 196624 | tf_op jit(solution)/shard_map/psum | solution.py:69
  146.4 1.4 convolution_bitcast_fusion.2
  147.9 1.5 collective-permute-start.3
  149.4 8.9 %collective-permute-done.3 = f32[256,384]{1,0:T(8,128)S(1)} collective-permute-done((f32[256,384]{1,0:T(8,128)S(1)}, f32[256,384]{1,0:T(8,128)S(1)}, u32[]{:S(2)}, u32[]{:S(2)}) %collective-permute-start.3) | collective-permute-done | bytes 393248 | tf_op jit(solution)/shard_map/ppermute | solution.py:12
  158.4 2.5 collective-permute-start.4
  160.9 16.4 %collective-permute-done.4 = f32[256,384]{1,0:T(8,128)S(1)} collective-permute-done((f32[256,384]{1,0:T(8,128)S(1)}, f32[256,384]{1,0:T(8,128)S(1)}, u32[]{:S(2)}, u32[]{:S(2)}) %collective-permute-start.4) | collective-permute-done | bytes 393248 | tf_op jit(solution)/shard_map/ppermute | solution.py:12
  177.3 2.2 fusion.7
  179.5 0.0 all-reduce.12.cloned.1.call-update
  179.5 0.2 all-reduce.14.cloned.1.call-start
  179.7 25.6 %all-reduce.12.cloned.1.call-done = f32[256,384]{0,1:T(8,128)} async-done(((f32[256,384]{0,1:T(8,128)}), f32[256,384]{0,1:T(8,128)}) %all-reduce.12.cloned.1.call-update) | async-done | bytes 393232 | tf_op jit(solution)/shard_map/psum | solution.py:92
  205.4 1.7 convolution_bitcast_fusion.1
  207.1 1.6 collective-permute-start.5
  208.7 1.7 convolution_multiply_fusion
  210.4 7.7 %collective-permute-done.5 = f32[256,384]{1,0:T(8,128)S(1)} collective-permute-done((f32[256,384]{1,0:T(8,128)S(1)}, f32[256,384]{1,0:T(8,128)S(1)}, u32[]{:S(2)}, u32[]{:S(2)}) %collective-permute-start.5) | collective-permute-done | bytes 393248 | tf_op jit(solution)/shard_map/ppermute | solution.py:12
  218.1 0.0 copy-start.3
  218.1 0.7 copy-done.3
  218.8 2.6 fusion.1
  221.4 0.0 all-reduce.14.cloned.1.call-update
  221.5 0.9 constant_dynamic-slice_fusion.1
  222.4 33.5 %all-reduce.14.cloned.1.call-done = f32[512,384]{1,0:T(8,128)} async-done(((f32[512,384]{1,0:T(8,128)}), f32[512,384]{1,0:T(8,128)}) %all-reduce.14.cloned.1.call-update) | async-done | bytes 786448 | tf_op jit(solution)/shard_map/psum | solution.py:92
  256.0 2.2 convolution_bitcast_fusion
  258.2 0.9 pad_maximum_fusion
  (20 shorter events, 0.2 us)
Async XLA Ops:
  6.5 3.2 %slice-start = ((f32[448,384]{1,0:T(8,128)}), f32[128,384]{1,0:T(8,128)S(1)}, s32[]{:S(2)}) async-start(f32[448,384]{1,0:T(8,128)} %param.4), calls=%async_computation.5 | async-start | bytes 393216 | tf_op jit(solution)/shard_map/slice | solution.py:60
  6.5 3.2 %copy-start.4 = (s32[1,3]{1,0:T(1,128)S(1)}, s32[1,3]{1,0:T(1,128)}, u32[]{:S(2)}) copy-start(s32[1,3]{1,0:T(1,128)} %param.7) | copy-start | bytes 40
  6.5 40.4 %all-reduce.6.cloned.1.call-start = ((), (), s32[]{:S(2)}) async-start(), calls=%async_computation | async-start | bytes 1572864 | tf_op jit(solution)/shard_map/psum | solution.py:69
  9.7 37.2 %copy-start.1 = (f32[1280,256]{1,0:T(8,128)S(1)}, f32[1280,256]{1,0:T(8,128)}, u32[]{:S(2)}) copy-start(f32[1280,256]{1,0:T(8,128)} %param.6) | copy-start | bytes 3932164
  9.7 78.6 %all-reduce.8.cloned.1.call-start = ((), (), s32[]{:S(2)}) async-start(), calls=%async_computation.1 | async-start | bytes 786432 | tf_op jit(solution)/shard_map/psum | solution.py:69
  10.6 50.5 %copy-start.2 = (f32[896,256]{1,0:T(8,128)S(1)}, f32[896,256]{1,0:T(8,128)}, u32[]{:S(2)}) copy-start(f32[896,256]{1,0:T(8,128)} %param.5) | copy-start | bytes 2752516
  50.1 12.3 %slice-start.1 = ((f32[448,384]{1,0:T(8,128)}), f32[64,384]{1,0:T(8,128)S(1)}, s32[]{:S(2)}) async-start(f32[448,384]{1,0:T(8,128)} %param.4), calls=%async_computation.6 | async-start | bytes 196608 | tf_op jit(solution)/shard_map/slice | solution.py:60
  50.1 10.9 %collective-permute-start = (f32[256,384]{0,1:T(8,128)S(1)}, f32[256,384]{0,1:T(8,128)S(1)}, u32[]{:S(2)}, u32[]{:S(2)}) collective-permute-start(f32[256,384]{0,1:T(8,128)S(1)} %fusion.3), channel_id=1, source_target_pairs={{0,4},{4,0},{8,12},{12,8},{1,5},{5,1},{9,13},{13,9},{2,6},{6,2},{1... | collective-permute-start | bytes 1179656 | tf_op jit(solution)/shard_map/ppermute | solution.py:12
  62.3 28.0 %copy-start = (f32[512,384]{1,0:T(8,128)S(1)}, f32[512,384]{1,0:T(8,128)}, u32[]{:S(2)}) copy-start(f32[512,384]{1,0:T(8,128)} %all-reduce.6.cloned.1.call-done) | copy-start | bytes 2359300
  62.4 84.1 %all-reduce.10.cloned.1.call-start = ((), (), s32[]{:S(2)}) async-start(), calls=%async_computation.2 | async-start | bytes 393216 | tf_op jit(solution)/shard_map/psum | solution.py:69
  92.4 10.9 %collective-permute-start.1 = (f32[256,384]{0,1:T(8,128)S(1)}, f32[256,384]{0,1:T(8,128)S(1)}, u32[]{:S(2)}, u32[]{:S(2)}) collective-permute-start(f32[256,384]{0,1:T(8,128)S(1)} %fusion.6), channel_id=1, source_target_pairs={{0,4},{4,0},{8,12},{12,8},{1,5},{5,1},{9,13},{13,9},{2,6},{6,2},{1... | collective-permute-start | bytes 1179656 | tf_op jit(solution)/shard_map/ppermute | solution.py:12
  103.4 19.4 %collective-permute-start.2 = (f32[256,384]{0,1:T(8,128)S(1)}, f32[256,384]{0,1:T(8,128)S(1)}, u32[]{:S(2)}, u32[]{:S(2)}) collective-permute-start(f32[256,384]{0,1:T(8,128)S(1)} %add.68), channel_id=1, source_target_pairs={{0,8},{4,12},{8,0},{12,4},{1,9},{5,13},{9,1},{13,5},{2,10},{6,14},... | collective-permute-start | bytes 1179656 | tf_op jit(solution)/shard_map/ppermute | solution.py:12
  124.0 81.4 %all-reduce.12.cloned.1.call-start = ((), (), s32[]{:S(2)}) async-start(), calls=%async_computation.3 | async-start | bytes 786432 | tf_op jit(solution)/shard_map/psum | solution.py:92
  147.9 10.5 %collective-permute-start.3 = (f32[256,384]{1,0:T(8,128)S(1)}, f32[256,384]{1,0:T(8,128)S(1)}, u32[]{:S(2)}, u32[]{:S(2)}) collective-permute-start(f32[256,384]{1,0:T(8,128)S(1)} %convolution_bitcast_fusion.2), channel_id=1, source_target_pairs={{0,4},{4,0},{8,12},{12,8},{1,5},{5,1},{9,13},{13,9},{2,6},{6,2},{1... | collective-permute-start | bytes 1179656 | tf_op jit(solution)/shard_map/ppermute | solution.py:12
  158.4 18.9 %collective-permute-start.4 = (f32[256,384]{1,0:T(8,128)S(1)}, f32[256,384]{1,0:T(8,128)S(1)}, u32[]{:S(2)}, u32[]{:S(2)}) collective-permute-start(f32[256,384]{1,0:T(8,128)S(1)} %add.70), channel_id=1, source_target_pairs={{0,8},{4,12},{8,0},{12,4},{1,9},{5,13},{9,1},{13,5},{2,10},{6,14},... | collective-permute-start | bytes 1179656 | tf_op jit(solution)/shard_map/ppermute | solution.py:12
  179.5 76.5 %all-reduce.14.cloned.1.call-start = ((), (), s32[]{:S(2)}) async-start(), calls=%async_computation.4 | async-start | bytes 1572864 | tf_op jit(solution)/shard_map/psum | solution.py:92
  207.1 10.9 %collective-permute-start.5 = (f32[256,384]{1,0:T(8,128)S(1)}, f32[256,384]{1,0:T(8,128)S(1)}, u32[]{:S(2)}, u32[]{:S(2)}) collective-permute-start(f32[256,384]{1,0:T(8,128)S(1)} %convolution_bitcast_fusion.1), channel_id=1, source_target_pairs={{0,4},{4,0},{8,12},{12,8},{1,5},{5,1},{9,13},{13,9},{2,6},{6,2},{1... | collective-permute-start | bytes 1179656 | tf_op jit(solution)/shard_map/ppermute | solution.py:12
  218.1 0.7 copy-start.3
Sparse Core Ops, SparseCore 0:
  9.8 37.0 all-reduce.5
  62.5 25.7 all-reduce.7
  124.1 22.2 all-reduce.9
  179.6 25.7 all-reduce.11
  221.6 34.3 all-reduce.13
where the time goes:
time: 266 us
  waiting for transfers between devices  209 us (79%)
  matrix products  24.8 us (9%)
  between operations  13.4 us (5%)
  starting transfers between devices  11.5 us (4%)
  local copies, waits for them, and re-layouts  5.43 us (2%)
    psum x3, waiting for transfers between devices, body(): solved_part = lax.psum(local_product, 'rows')  81.6 us
    ppermute x6, waiting for transfers between devices, partner(): return lax.ppermute(value, axis, pairs)  68.6 us
    psum x2, waiting for transfers between devices, body(): remainder = remainder - lax.psum(partial_value, 'rows')  59.2 us
    dot_general x6, matrix products, contract_rows(): lax.dot_general(matrix, vectors, (((0,), (0,)), ((), ())), precision=lax....  12.8 us
    ppermute x6, starting transfers between devices, partner(): return lax.ppermute(value, axis, pairs)  11.2 us
    dot_general x3, matrix products, body(): jnp.dot(coupling, answers[upper_level], precision=highest, preferred_elem...  6.48 us
    dot_general x3, matrix products, body(): jnp.dot(inverse_block, reduced, precision=highest, preferred_element_type...  5.54 us
  transfers between devices with their start and end apart: 11, of which 11 were waited for; matrix products, arithmetic and copies ran while one was open for 2% of the time, Pallas kernels for 0%

commit v1 on v0

--- a/solution.py
+++ b/solution.py
@@ -1,6 +1,8 @@
 import jax
 import jax.numpy as jnp
 from jax import lax
+from jax.experimental import pallas as pl
+from jax.experimental.pallas import tpu as pltpu
 from jax.sharding import PartitionSpec as P
 
 S = 512
@@ -100,7 +102,228 @@
     return jnp.concatenate(pieces, axis=0)
 
 
+F32 = jnp.float32
+NT = (((1,), (1,)), ((), ()))
+NN = (((1,), (0,)), ((), ()))
+
+
+def split_two(a):
+    hi = a.astype(jnp.bfloat16)
+    return hi, (a - hi.astype(F32)).astype(jnp.bfloat16)
+
+
+def dot3(a, b, dims):
+    ah, al = split_two(a)
+    bh, bl = split_two(b)
+    one = lambda u, v: lax.dot_general(u, v, dims, preferred_element_type=F32)
+    return one(ah, bh) + (one(ah, bl) + one(al, bh))
+
+
+def kernel(
+    rhs_ref, dinv_ref, lower_ref, pat_ref, out_ref,
+    xd, xl, b12, zd, zl, d2, turned, rturned, y0, e1, e2, g1, g2, y1, g3, f2,
+    s2, v1, v2, v0, ot, send_sem, recv_sem,
+):
+    r = lax.axis_index("rows")
+    j = lax.axis_index("leaf")
+    k = lax.axis_index("rhs")
+    b0, b1 = j % 2, j // 2
+    z0 = j + 1 - 2 * b0
+    z1 = (j + 2) % 4
+    z3 = (z0 + 2) % 4
+    xp, kp = {"rows": 1 - r}, {"rhs": 1 - k}
+    Z0, Z1, Z3 = {"leaf": z0}, {"leaf": z1}, {"leaf": z3}
+    barrier = pltpu.get_barrier_semaphore()
+    for peer in (xp, kp, Z0, Z1, Z3):
+        pl.semaphore_signal(barrier, inc=1, device_id=peer, device_id_type=pl.DeviceIdType.MESH)
+    pl.semaphore_wait(barrier, 5)
+
+    sent = []
+
+    def send(src, dst, peer):
+        n = len(sent)
+        copy = pltpu.make_async_remote_copy(
+            src_ref=src, dst_ref=dst, send_sem=send_sem.at[n], recv_sem=recv_sem.at[n],
+            device_id=peer, device_id_type=pl.DeviceIdType.MESH,
+        )
+        copy.start()
+        sent.append(copy)
+        return copy
+
+    def part(start, rows):
+        half = rows // 2
+        return pl.ds(pl.multiple_of(start + k * half, 8), half)
+
+    def hop(src, s_start, dst, d_start, rows, peer):
+        return send(src.at[part(s_start, rows)], dst.at[part(d_start, rows)], peer)
+
+    def share(copy, dst, d_start, rows):
+        copy.wait_recv()
+        return send(dst.at[part(d_start, rows)], dst.at[part(d_start, rows)], kp)
+
+    h_d0 = hop(dinv_ref, 0, xd, 0, 512, xp)
+    m01 = pat_ref[0, 0].astype(F32)
+    m02 = pat_ref[0, 1].astype(F32)
+    b12[0] = lower_ref[1024:1280] * pat_ref[0, 2].astype(F32)
+    d2[0, 0:128] = dinv_ref[768:896]
+    for c in range(0, 384, 128):
+        for q in (0, 128, 256):
+            turned[c : c + 128, q : q + 128] = rhs_ref[q : q + 128, c : c + 128].T
+        last = rhs_ref[384:448, c : c + 128]
+        turned[c : c + 128, 384:512] = jnp.concatenate([last, last], axis=0).T
+    theirs = pl.ds(pl.multiple_of((1 - r) * 192, 8), 192)
+    mine = pl.ds(pl.multiple_of(r * 192, 8), 192)
+    q_a = send(turned.at[theirs, 0:256], rturned.at[:, 0:256], xp)
+    h_b01 = hop(lower_ref, 0, xl, 0, 512, xp)
+    z_d1 = hop(dinv_ref, 512, zd.at[0], 0, 256, Z0)
+    z_b12 = hop(b12.at[0], 0, zl.at[0], 0, 256, Z0)
+    h_d1 = hop(dinv_ref, 512, xd, 512, 256, xp)
+    q_b = send(turned.at[theirs, 256:512], rturned.at[:, 256:512], xp)
+    h_b02 = hop(lower_ref, 512, xl, 512, 512, xp)
+    h_b12 = hop(b12.at[0], 0, b12.at[1], 0, 256, xp)
+    h_d2 = hop(d2.at[0], 0, d2.at[1], 0, 128, xp)
+    z_d2 = [hop(d2.at[0], 0, d2.at[0], 128 * (i + 1), 128, Z) for i, Z in enumerate((Z0, Z1, Z3))]
+
+    s_d0 = share(h_d0, xd, 0, 512)
+    q_a.wait_recv()
+    y_own = dot3(turned[mine, 0:256], dinv_ref[0:512], NT)
+    s_d0.wait_recv()
+    y0[...] = y_own + dot3(rturned[:, 0:256], xd[0:512], NT)
+
+    s_b01 = share(h_b01, xl, 0, 512)
+    lane = lax.broadcasted_iota(jnp.int32, (192, 256), 1)
+    q_b.wait_recv()
+
+    def own_rows(h, level):
+        v = (turned[mine, 256:512], rturned[:, 256:512])[h]
+        v = v[:, 0:128] if level == 1 else v[:, 128:256]
+        wide = jnp.concatenate([v, v], axis=1)
+        where = (lane // 128 == b0) if level == 1 else (lane // 64 == j)
+        return jnp.where(where, wide, 0.0)
+
+    keep96 = pl.ds(pl.multiple_of(b0 * 96, 8), 96)
+    give96 = pl.ds(pl.multiple_of((1 - b0) * 96, 8), 96)
+    keep48 = pl.ds(pl.multiple_of(b1 * 48, 8), 48)
+    give48 = pl.ds(pl.multiple_of((1 - b1) * 48, 8), 48)
+
+    e1[0] = own_rows(0, 1) - m01 * dot3(y0[...], lower_ref[0:512], NN)
+    s_b01.wait_recv()
+    e1[1] = own_rows(1, 1) - m01 * dot3(y0[...], xl[0:512], NN)
+    c_1 = send(e1.at[:, give96], g1, Z0)
+
+    s_zd1 = share(z_d1, zd.at[0], 0, 256)
+    s_d1 = share(h_d1, xd, 512, 256)
+    z_xd1 = hop(xd, 512, zd.at[1], 0, 256, Z0)
+    s_zb12 = share(z_b12, zl.at[0], 0, 256)
+    e2[0] = own_rows(0, 2) - m02 * dot3(y0[...], lower_ref[512:1024], NN)
+    s_b02 = share(h_b02, xl, 512, 512)
+    s_xd1 = share(z_xd1, zd.at[1], 0, 256)
+    s_b02.wait_recv()
+    e2[1] = own_rows(1, 2) - m02 * dot3(y0[...], xl[512:1024], NN)
+    c_2 = send(e2.at[:, give96], g2, Z0)
+    s_b12 = share(h_b12, b12.at[1], 0, 256)
+    z_xb12 = hop(b12.at[1], 0, zl.at[1], 0, 256, Z0)
+    s_d2 = share(h_d2, d2.at[1], 0, 128)
+    z_xd2 = [hop(d2.at[1], 0, d2.at[1], 128 * (i + 1), 128, Z) for i, Z in enumerate((Z0, Z1, Z3))]
+    s_zd2 = [share(z, d2.at[0], 128 * (i + 1), 128) for i, z in enumerate(z_d2)]
+
+    c_1.wait_recv()
+    c1 = [e1[h, keep96] + g1[h] for h in range(2)]
+    s_d1.wait_recv()
+    y1[0] = dot3(c1[0], dinv_ref[512:768], NT) + dot3(c1[1], xd[512:768], NT)
+    s_zd1.wait_recv()
+    s_xd1.wait_recv()
+    y1[1] = dot3(c1[0], zd[0], NT) + dot3(c1[1], zd[1], NT)
+    s_xb12 = share(z_xb12, zl.at[1], 0, 256)
+    s_zb12.wait_recv()
+    s_b12.wait_recv()
+    c_2.wait_recv()
+    s_xb12.wait_recv()
+    for h in range(2):
+        up = dot3(y1[0], b12[h], NN) + dot3(y1[1], zl[h], NN)
+        f2[h] = e2[h, keep96] + g2[h] - up
+    c_3 = send(f2.at[:, give48], g3, Z1)
+    s_xzd2 = [share(z, d2.at[1], 128 * (i + 1), 128) for i, z in enumerate(z_xd2)]
+
+    for s in [s_d2] + s_zd2 + s_xzd2:
+        s.wait_recv()
+    c_3.wait_recv()
+    y2 = dot3(f2[0, keep48] + g3[0], d2[0], NT) + dot3(f2[1, keep48] + g3[1], d2[1], NT)
+    for h in range(2):
+        s2[h] = dot3(y2, d2[h], NN)
+    at48 = pl.ds(pl.multiple_of(b0 * 96 + b1 * 48, 8), 48)
+    v2[:, at48] = s2[...]
+    a_2 = send(s2, v2.at[:, at48], Z1)
+    a_2.wait_recv()
+    at96 = keep96
+    b_2 = send(v2.at[:, at96], v2.at[:, at96], Z0)
+
+    x2 = [v2[h, at96] for h in range(2)]
+    r1 = [
+        y1[0] - dot3(x2[0], b12[0], NT) - dot3(x2[1], b12[1], NT),
+        y1[1] - dot3(x2[0], zl[0], NT) - dot3(x2[1], zl[1], NT),
+    ]
+    v1[0, at96] = dot3(r1[0], dinv_ref[512:768], NN) + dot3(r1[1], zd[0], NN)
+    v1[1, at96] = dot3(r1[0], xd[512:768], NN) + dot3(r1[1], zd[1], NN)
+    b_1 = send(v1.at[:, at96], v1.at[:, at96], Z0)
+    b_2.wait_recv()
+    l1 = pl.ds(pl.multiple_of(b0 * 128, 128), 128)
+    l2 = pl.ds(pl.multiple_of(b1 * 128, 128), 128)
+    o_2 = send(v2.at[1, :, l2], ot.at[mine, 384:512], xp)
+    t = m02 * (dot3(v2[0], lower_ref[512:1024], NT) + dot3(v2[1], xl[512:1024], NT))
+    y0[...] = y0[...] - t
+    b_1.wait_recv()
+    o_1 = send(v1.at[1, :, l1], ot.at[mine, 256:384], xp)
+
+    t = m01 * (dot3(v1[0], lower_ref[0:512], NT) + dot3(v1[1], xl[0:512], NT))
+    y0[...] = y0[...] - t
+    v0[...] = dot3(y0[...], xd[0:512], NN)
+    o_0 = send(v0, ot.at[mine, 0:256], xp)
+    ot[mine, 0:256] = dot3(y0[...], dinv_ref[0:512], NN)
+    ot[mine, 256:384] = v1[0, :, l1]
+    ot[mine, 384:512] = v2[0, :, l2]
+    o_2.wait_recv()
+    o_1.wait_recv()
+    for c in range(0, 384, 128):
+        out_ref[256:384, c : c + 128] = ot[c : c + 128, 256:384].T
+        both = ot[c : c + 128, 384:512].T
+        out_ref[384:448, c : c + 128] = jnp.where(b0 == 0, both[0:64], both[64:128])
+    o_0.wait_recv()
+    for c in range(0, 384, 128):
+        for q in (0, 128):
+            out_ref[q : q + 128, c : c + 128] = ot[c : c + 128, q : q + 128].T
+    for copy in sent:
+        copy.wait_send()
+
+
+MESSAGES = 64
+
+
+def fused(rhs, dinv, lower, pattern):
+    vm = lambda *shape: pltpu.VMEM(shape, F32)
+    whole = pl.BlockSpec(memory_space=pltpu.VMEM)
+    return pl.pallas_call(
+        kernel,
+        out_shape=jax.ShapeDtypeStruct(rhs.shape, F32),
+        in_specs=[whole, whole, whole, pl.BlockSpec(memory_space=pltpu.SMEM)],
+        out_specs=whole,
+        scratch_shapes=[
+            vm(896, 256), vm(1024, 256), vm(2, 256, 256), vm(2, 256, 256), vm(2, 256, 256),
+            vm(2, 512, 256), vm(384, 512), vm(192, 512), vm(192, 512), vm(2, 192, 256),
+            vm(2, 192, 256), vm(2, 96, 256), vm(2, 96, 256), vm(2, 96, 256), vm(2, 48, 256),
+            vm(2, 96, 256), vm(2, 48, 256), vm(2, 192, 256), vm(2, 192, 256), vm(192, 256), vm(384, 512),
+            pltpu.SemaphoreType.DMA((MESSAGES,)),
+            pltpu.SemaphoreType.DMA((MESSAGES,)),
+        ],
+        compiler_params=pltpu.CompilerParams(
+            collective_id=0, has_side_effects=True, vmem_limit_bytes=48 * 2**20
+        ),
+    )(rhs, dinv, lower, pattern)
+
+
 def solution(mesh):
+    sizes = mesh.shape
+    small = sizes["leaf"] == 4 and sizes["rows"] == 2 and sizes["rhs"] == 2
     placed = (
         P(("groups", "leaf", "rows"), "rhs"),
         P(("groups", "leaf"), "rows"),
@@ -108,7 +331,7 @@
         P(("groups", "leaf"), None),
     )
     return jax.shard_map(
-        body,
+        fused if small else body,
         mesh=mesh,
         in_specs=placed,
         out_specs=P(("groups", "leaf", "rows"), "rhs"),

time: 266 us -> 85.9 us (0.32)
  waiting for transfers between devices: 209 us -> 0 us
  Pallas kernels: 0 us -> 80.5 us
  matrix products: 24.8 us -> 0 us
  between operations: 13.4 us -> 0.01 us
  starting transfers between devices: 11.5 us -> 0 us
    psum x5 -> x0, waiting for transfers between devices: 141 us -> none  [the longest x3 81.6 us: body(): solved_part = lax.psum(local_product, 'rows')]
    pallas_call x0 -> x1, Pallas kernels: none -> 80.5 us  [fused(): pl.pallas_call(kernel, out_shape=jax.ShapeDtypeStruct(rhs.shape, F32), in...]
    ppermute x6 -> x0, waiting for transfers between devices: 68.6 us -> none  [partner(): return lax.ppermute(value, axis, pairs)]
    dot_general x12 -> x0, matrix products: 24.8 us -> none  [the longest x6 12.8 us: contract_rows(): lax.dot_general(matrix, vectors, (((0,), (0,)), ((), ())), precision=lax....]
    ppermute x6 -> x0, starting transfers between devices: 11.2 us -> none  [partner(): return lax.ppermute(value, axis, pairs)]
    unnamed x12 -> x9, local copies, waits for them, and re-layouts: 1.7 us -> 5.1 us
  transfers between devices with their start and end apart: 11 -> 0, of which waited for: 11 -> 0; matrix products, arithmetic and copies ran while one was open for 2% -> 0% of each run, Pallas kernels for 0% -> 0%
where the time goes in v1:
time: 85.9 us; the launch traced here: 85.7 us
  Pallas kernels  80.5 us (94%)
  local copies, waits for them, and re-layouts  5.1 us (6%)
    pallas_call x1, Pallas kernels, fused(): pl.pallas_call(kernel, out_shape=jax.ShapeDtypeStruct(rhs.shape, F32), in...  80.5 us
    unnamed x9, local copies, waits for them, and re-layouts  5.1 us

profile of v1, /device:TPU:0, one launch (start us, length us, event | category | flops | bytes accessed | tf_op | source)
XLA Modules:
  0.0 85.7 jit_solution(11077585785382437769)
XLA Ops:
  0.0 0.0 copy-start
  0.0 1.3 %copy-done = f32[1280,256]{1,0:T(8,128)S(1)} copy-done((f32[1280,256]{1,0:T(8,128)S(1)}, f32[1280,256]{1,0:T(8,128)}, u32[]{:S(2)}) %copy-start) | copy-done | bytes 1310744
  1.3 0.0 copy-start.1
  1.3 1.2 %copy-done.1 = f32[896,256]{1,0:T(8,128)S(1)} copy-done((f32[896,256]{1,0:T(8,128)S(1)}, f32[896,256]{1,0:T(8,128)}, u32[]{:S(2)}) %copy-start.1) | copy-done | bytes 917528
  2.5 0.0 copy-start.2
  2.5 1.1 %copy-done.2 = f32[448,384]{1,0:T(8,128)S(1)} copy-done((f32[448,384]{1,0:T(8,128)S(1)}, f32[448,384]{1,0:T(8,128)}, u32[]{:S(2)}) %copy-start.2) | copy-done | bytes 688152
  3.6 0.0 copy-start.3
  3.6 0.7 copy-done.3
  4.3 80.5 %shard_map.46 = f32[448,384]{1,0:T(8,128)S(1)} custom-call(f32[448,384]{1,0:T(8,128)S(1)} %copy-done.2, f32[896,256]{1,0:T(8,128)S(1)} %copy-done.1, f32[1280,256]{1,0:T(8,128)S(1)} %copy-done, s32[1,3]{1,0:T(1,128)S(1)} %copy-done.3), custom_call_target="tpu_custom_call" | custom-call | tf_op jit(solution)/shard_map/pallas_call | solution.py:305
  84.8 0.8 copy.6
Async XLA Ops:
  0.0 1.3 %copy-start = (f32[1280,256]{1,0:T(8,128)S(1)}, f32[1280,256]{1,0:T(8,128)}, u32[]{:S(2)}) copy-start(f32[1280,256]{1,0:T(8,128)} %lower_ref.1) | copy-start | bytes 3932164
  1.3 1.2 %copy-start.1 = (f32[896,256]{1,0:T(8,128)S(1)}, f32[896,256]{1,0:T(8,128)}, u32[]{:S(2)}) copy-start(f32[896,256]{1,0:T(8,128)} %dinv_ref.1) | copy-start | bytes 2752516
  2.5 1.1 %copy-start.2 = (f32[448,384]{1,0:T(8,128)S(1)}, f32[448,384]{1,0:T(8,128)}, u32[]{:S(2)}) copy-start(f32[448,384]{1,0:T(8,128)} %rhs_ref.1) | copy-start | bytes 2064388
  3.6 0.7 copy-start.3

commit v2 on v1

--- a/solution.py
+++ b/solution.py
@@ -120,9 +120,9 @@
 
 
 def kernel(
-    rhs_ref, dinv_ref, lower_ref, pat_ref, out_ref,
-    xd, xl, b12, zd, zl, d2, turned, rturned, y0, e1, e2, g1, g2, y1, g3, f2,
-    s2, v1, v2, v0, ot, send_sem, recv_sem,
+    rhs_hbm, dinv_hbm, lower_hbm, pat_ref, out_ref,
+    rhs_ref, dinv_ref, lower_ref, xd, xl, b12, zd, zl, d2, turned, rturned, y0, e1, e2,
+    g1, g2, u1, u2, y1, g3, f2, s2, v1, v2, ob, ot, load_sem, send_sem, recv_sem,
 ):
     r = lax.axis_index("rows")
     j = lax.axis_index("leaf")
@@ -136,6 +136,14 @@
     barrier = pltpu.get_barrier_semaphore()
     for peer in (xp, kp, Z0, Z1, Z3):
         pl.semaphore_signal(barrier, inc=1, device_id=peer, device_id_type=pl.DeviceIdType.MESH)
+    loads = [
+        pltpu.make_async_copy(src, dst, load_sem.at[n])
+        for n, (src, dst) in enumerate(
+            ((rhs_hbm, rhs_ref), (dinv_hbm, dinv_ref), (lower_hbm, lower_ref))
+        )
+    ]
+    for load in loads:
+        load.start()
     pl.semaphore_wait(barrier, 5)
 
     sent = []
@@ -161,87 +169,93 @@
         copy.wait_recv()
         return send(dst.at[part(d_start, rows)], dst.at[part(d_start, rows)], kp)
 
-    h_d0 = hop(dinv_ref, 0, xd, 0, 512, xp)
-    m01 = pat_ref[0, 0].astype(F32)
-    m02 = pat_ref[0, 1].astype(F32)
-    b12[0] = lower_ref[1024:1280] * pat_ref[0, 2].astype(F32)
-    d2[0, 0:128] = dinv_ref[768:896]
+    def rows_at(start, size):
+        return pl.ds(pl.multiple_of(start, 8), size)
+
+    keep192, give192 = rows_at(b0 * 192, 192), rows_at((1 - b0) * 192, 192)
+    keep96, give96 = rows_at(r * 96, 96), rows_at((1 - r) * 96, 96)
+    keep48, give48 = rows_at(b1 * 48, 48), rows_at((1 - b1) * 48, 48)
+    at96, off96 = rows_at(b0 * 96, 96), rows_at((1 - b0) * 96, 96)
+    at48 = rows_at(b0 * 96 + b1 * 48, 48)
+
+    h_d0 = hop(dinv_hbm, 0, xd, 0, 512, xp)
+    loads[0].wait()
     for c in range(0, 384, 128):
         for q in (0, 128, 256):
             turned[c : c + 128, q : q + 128] = rhs_ref[q : q + 128, c : c + 128].T
         last = rhs_ref[384:448, c : c + 128]
         turned[c : c + 128, 384:512] = jnp.concatenate([last, last], axis=0).T
-    theirs = pl.ds(pl.multiple_of((1 - r) * 192, 8), 192)
-    mine = pl.ds(pl.multiple_of(r * 192, 8), 192)
-    q_a = send(turned.at[theirs, 0:256], rturned.at[:, 0:256], xp)
-    h_b01 = hop(lower_ref, 0, xl, 0, 512, xp)
-    z_d1 = hop(dinv_ref, 512, zd.at[0], 0, 256, Z0)
+    q_a = send(turned.at[give192, 0:256], rturned.at[give192], xp)
+    q_b = send(turned.at[keep192, 0:256], rturned.at[keep192], xp)
+    m01 = pat_ref[0, 0].astype(F32)
+    m02 = pat_ref[0, 1].astype(F32)
+    z_d1 = hop(dinv_hbm, 512, zd.at[0], 0, 256, Z0)
+    loads[1].wait()
+    loads[2].wait()
+    b12[0] = lower_ref[1024:1280] * pat_ref[0, 2].astype(F32)
+    d2[0, 0:128] = dinv_ref[768:896]
     z_b12 = hop(b12.at[0], 0, zl.at[0], 0, 256, Z0)
-    h_d1 = hop(dinv_ref, 512, xd, 512, 256, xp)
-    q_b = send(turned.at[theirs, 256:512], rturned.at[:, 256:512], xp)
-    h_b02 = hop(lower_ref, 512, xl, 512, 512, xp)
+    z_d2 = [hop(d2.at[0], 0, d2.at[0], 128 * (i + 1), 128, Z) for i, Z in enumerate((Z0, Z1, Z3))]
+
+    lane = lax.broadcasted_iota(jnp.int32, (192, 256), 1)
+
+    def own_rows(half, level):
+        v = turned[half, 256:384] if level == 1 else turned[half, 384:512]
+        where = (lane // 128 == b0) if level == 1 else (lane // 64 == j)
+        return jnp.where(where, jnp.concatenate([v, v], axis=1), 0.0)
+
+    y0[give192] = dot3(turned[give192, 0:256], dinv_ref[0:512], NT)
+    s_d0 = share(h_d0, xd, 0, 512)
+    y0[keep192] = dot3(turned[keep192, 0:256], dinv_ref[0:512], NT)
+    q_a.wait_recv()
+    s_d0.wait_recv()
+    y = y0[give192] + dot3(rturned[give192], xd[0:512], NT)
+    y0[give192] = y
+    e1[0] = own_rows(give192, 1) - m01 * dot3(y, lower_ref[0:512], NN)
+    c_1 = send(e1.at[0], g1, Z0)
+    e2[0] = own_rows(give192, 2) - m02 * dot3(y, lower_ref[512:1024], NN)
+    c_2 = send(e2.at[0], g2, Z0)
+    h_d1 = hop(dinv_hbm, 512, xd, 512, 256, xp)
+    s_zd1 = share(z_d1, zd.at[0], 0, 256)
+    s_zb12 = share(z_b12, zl.at[0], 0, 256)
+    q_b.wait_recv()
     h_b12 = hop(b12.at[0], 0, b12.at[1], 0, 256, xp)
-    h_d2 = hop(d2.at[0], 0, d2.at[1], 0, 128, xp)
-    z_d2 = [hop(d2.at[0], 0, d2.at[0], 128 * (i + 1), 128, Z) for i, Z in enumerate((Z0, Z1, Z3))]
-
-    s_d0 = share(h_d0, xd, 0, 512)
-    q_a.wait_recv()
-    y_own = dot3(turned[mine, 0:256], dinv_ref[0:512], NT)
-    s_d0.wait_recv()
-    y0[...] = y_own + dot3(rturned[:, 0:256], xd[0:512], NT)
-
-    s_b01 = share(h_b01, xl, 0, 512)
-    lane = lax.broadcasted_iota(jnp.int32, (192, 256), 1)
-    q_b.wait_recv()
-
-    def own_rows(h, level):
-        v = (turned[mine, 256:512], rturned[:, 256:512])[h]
-        v = v[:, 0:128] if level == 1 else v[:, 128:256]
-        wide = jnp.concatenate([v, v], axis=1)
-        where = (lane // 128 == b0) if level == 1 else (lane // 64 == j)
-        return jnp.where(where, wide, 0.0)
-
-    keep96 = pl.ds(pl.multiple_of(b0 * 96, 8), 96)
-    give96 = pl.ds(pl.multiple_of((1 - b0) * 96, 8), 96)
-    keep48 = pl.ds(pl.multiple_of(b1 * 48, 8), 48)
-    give48 = pl.ds(pl.multiple_of((1 - b1) * 48, 8), 48)
-
-    e1[0] = own_rows(0, 1) - m01 * dot3(y0[...], lower_ref[0:512], NN)
-    s_b01.wait_recv()
-    e1[1] = own_rows(1, 1) - m01 * dot3(y0[...], xl[0:512], NN)
-    c_1 = send(e1.at[:, give96], g1, Z0)
-
-    s_zd1 = share(z_d1, zd.at[0], 0, 256)
+    y = y0[keep192] + dot3(rturned[keep192], xd[0:512], NT)
+    y0[keep192] = y
+    e1[1] = own_rows(keep192, 1) - m01 * dot3(y, lower_ref[0:512], NN)
+    e2[1] = own_rows(keep192, 2) - m02 * dot3(y, lower_ref[512:1024], NN)
     s_d1 = share(h_d1, xd, 512, 256)
     z_xd1 = hop(xd, 512, zd.at[1], 0, 256, Z0)
-    s_zb12 = share(z_b12, zl.at[0], 0, 256)
-    e2[0] = own_rows(0, 2) - m02 * dot3(y0[...], lower_ref[512:1024], NN)
-    s_b02 = share(h_b02, xl, 512, 512)
-    s_xd1 = share(z_xd1, zd.at[1], 0, 256)
-    s_b02.wait_recv()
-    e2[1] = own_rows(1, 2) - m02 * dot3(y0[...], xl[512:1024], NN)
-    c_2 = send(e2.at[:, give96], g2, Z0)
+    c_1.wait_recv()
+    e1[1] = e1[1] + g1[...]
+    t_1 = send(e1.at[1, give96], u1, xp)
+    h_d2 = hop(d2.at[0], 0, d2.at[1], 0, 128, xp)
     s_b12 = share(h_b12, b12.at[1], 0, 256)
     z_xb12 = hop(b12.at[1], 0, zl.at[1], 0, 256, Z0)
+    c_2.wait_recv()
+    e2[1] = e2[1] + g2[...]
+    t_2 = send(e2.at[1, give96], u2, xp)
+    h_b02 = hop(lower_hbm, 512, xl, 512, 512, xp)
+    h_b01 = hop(lower_hbm, 0, xl, 0, 512, xp)
+    s_zd2 = [share(z, d2.at[0], 128 * (i + 1), 128) for i, z in enumerate(z_d2)]
+
+    s_xd1 = share(z_xd1, zd.at[1], 0, 256)
+    t_1.wait_recv()
+    c1 = [e1[1, keep96], u1[...]]
+    s_d1.wait_recv()
+    y1[0] = dot3(c1[0], dinv_ref[512:768], NT) + dot3(c1[1], xd[512:768], NT)
     s_d2 = share(h_d2, d2.at[1], 0, 128)
     z_xd2 = [hop(d2.at[1], 0, d2.at[1], 128 * (i + 1), 128, Z) for i, Z in enumerate((Z0, Z1, Z3))]
-    s_zd2 = [share(z, d2.at[0], 128 * (i + 1), 128) for i, z in enumerate(z_d2)]
-
-    c_1.wait_recv()
-    c1 = [e1[h, keep96] + g1[h] for h in range(2)]
-    s_d1.wait_recv()
-    y1[0] = dot3(c1[0], dinv_ref[512:768], NT) + dot3(c1[1], xd[512:768], NT)
     s_zd1.wait_recv()
     s_xd1.wait_recv()
     y1[1] = dot3(c1[0], zd[0], NT) + dot3(c1[1], zd[1], NT)
     s_xb12 = share(z_xb12, zl.at[1], 0, 256)
     s_zb12.wait_recv()
+    t_2.wait_recv()
+    f2[0] = e2[1, keep96] - dot3(y1[0], b12[0], NN) - dot3(y1[1], zl[0], NN)
     s_b12.wait_recv()
-    c_2.wait_recv()
     s_xb12.wait_recv()
-    for h in range(2):
-        up = dot3(y1[0], b12[h], NN) + dot3(y1[1], zl[h], NN)
-        f2[h] = e2[h, keep96] + g2[h] - up
+    f2[1] = u2[...] - dot3(y1[0], b12[1], NN) - dot3(y1[1], zl[1], NN)
     c_3 = send(f2.at[:, give48], g3, Z1)
     s_xzd2 = [share(z, d2.at[1], 128 * (i + 1), 128) for i, z in enumerate(z_xd2)]
 
@@ -251,12 +265,13 @@
     y2 = dot3(f2[0, keep48] + g3[0], d2[0], NT) + dot3(f2[1, keep48] + g3[1], d2[1], NT)
     for h in range(2):
         s2[h] = dot3(y2, d2[h], NN)
-    at48 = pl.ds(pl.multiple_of(b0 * 96 + b1 * 48, 8), 48)
+    a_2 = send(s2, v2.at[:, at48], Z1)
+    b_2 = send(s2, v2.at[:, at48], Z0)
     v2[:, at48] = s2[...]
-    a_2 = send(s2, v2.at[:, at48], Z1)
+    s_b02 = share(h_b02, xl, 512, 512)
     a_2.wait_recv()
-    at96 = keep96
-    b_2 = send(v2.at[:, at96], v2.at[:, at96], Z0)
+    other48 = rows_at(b0 * 96 + (1 - b1) * 48, 48)
+    b_3 = send(v2.at[:, other48], v2.at[:, other48], Z0)
 
     x2 = [v2[h, at96] for h in range(2)]
     r1 = [
@@ -266,29 +281,45 @@
     v1[0, at96] = dot3(r1[0], dinv_ref[512:768], NN) + dot3(r1[1], zd[0], NN)
     v1[1, at96] = dot3(r1[0], xd[512:768], NN) + dot3(r1[1], zd[1], NN)
     b_1 = send(v1.at[:, at96], v1.at[:, at96], Z0)
-    b_2.wait_recv()
+    s_b01 = share(h_b01, xl, 0, 512)
+
     l1 = pl.ds(pl.multiple_of(b0 * 128, 128), 128)
     l2 = pl.ds(pl.multiple_of(b1 * 128, 128), 128)
-    o_2 = send(v2.at[1, :, l2], ot.at[mine, 384:512], xp)
-    t = m02 * (dot3(v2[0], lower_ref[512:1024], NT) + dot3(v2[1], xl[512:1024], NT))
-    y0[...] = y0[...] - t
+    arriving = []
+
+    def upper_out(n, block, rows):
+        ob[n, :, 256:384] = v1[1, block, l1]
+        ob[n, :, 384:512] = v2[1, block, l2]
+        arriving.append(send(ob.at[n, :, 256:512], ot.at[rows, 256:512], xp))
+        ot[rows, 256:384] = v1[0, block, l1]
+        ot[rows, 384:512] = v2[0, block, l2]
+
+    def lowest(n, block, rows):
+        t2 = dot3(v2[0, block], lower_ref[512:1024], NT) + dot3(v2[1, block], xl[512:1024], NT)
+        t1 = dot3(v1[0, block], lower_ref[0:512], NT) + dot3(v1[1, block], xl[0:512], NT)
+        rest = y0[rows] - m02 * t2 - m01 * t1
+        ob[n, :, 0:256] = dot3(rest, xd[0:512], NN)
+        arriving.append(send(ob.at[n, :, 0:256], ot.at[rows, 0:256], xp))
+        ot[rows, 0:256] = dot3(rest, dinv_ref[0:512], NN)
+
+    near, far = rows_at(b0 * 192 + r * 96, 96), rows_at((1 - b0) * 192 + r * 96, 96)
+    upper_out(0, at96, near)
+    s_b02.wait_recv()
+    s_b01.wait_recv()
+    lowest(0, at96, near)
+    b_2.wait_recv()
+    b_3.wait_recv()
     b_1.wait_recv()
-    o_1 = send(v1.at[1, :, l1], ot.at[mine, 256:384], xp)
-
-    t = m01 * (dot3(v1[0], lower_ref[0:512], NT) + dot3(v1[1], xl[0:512], NT))
-    y0[...] = y0[...] - t
-    v0[...] = dot3(y0[...], xd[0:512], NN)
-    o_0 = send(v0, ot.at[mine, 0:256], xp)
-    ot[mine, 0:256] = dot3(y0[...], dinv_ref[0:512], NN)
-    ot[mine, 256:384] = v1[0, :, l1]
-    ot[mine, 384:512] = v2[0, :, l2]
-    o_2.wait_recv()
-    o_1.wait_recv()
+    upper_out(1, off96, far)
+    lowest(1, off96, far)
+    arriving[0].wait_recv()
+    arriving[2].wait_recv()
     for c in range(0, 384, 128):
         out_ref[256:384, c : c + 128] = ot[c : c + 128, 256:384].T
         both = ot[c : c + 128, 384:512].T
         out_ref[384:448, c : c + 128] = jnp.where(b0 == 0, both[0:64], both[64:128])
-    o_0.wait_recv()
+    arriving[1].wait_recv()
+    arriving[3].wait_recv()
     for c in range(0, 384, 128):
         for q in (0, 128):
             out_ref[q : q + 128, c : c + 128] = ot[c : c + 128, q : q + 128].T
@@ -302,16 +333,20 @@
 def fused(rhs, dinv, lower, pattern):
     vm = lambda *shape: pltpu.VMEM(shape, F32)
     whole = pl.BlockSpec(memory_space=pltpu.VMEM)
+    hbm = pl.BlockSpec(memory_space=pltpu.HBM)
     return pl.pallas_call(
         kernel,
         out_shape=jax.ShapeDtypeStruct(rhs.shape, F32),
-        in_specs=[whole, whole, whole, pl.BlockSpec(memory_space=pltpu.SMEM)],
+        in_specs=[hbm, hbm, hbm, pl.BlockSpec(memory_space=pltpu.SMEM)],
         out_specs=whole,
         scratch_shapes=[
-            vm(896, 256), vm(1024, 256), vm(2, 256, 256), vm(2, 256, 256), vm(2, 256, 256),
-            vm(2, 512, 256), vm(384, 512), vm(192, 512), vm(192, 512), vm(2, 192, 256),
-            vm(2, 192, 256), vm(2, 96, 256), vm(2, 96, 256), vm(2, 96, 256), vm(2, 48, 256),
-            vm(2, 96, 256), vm(2, 48, 256), vm(2, 192, 256), vm(2, 192, 256), vm(192, 256), vm(384, 512),
+            vm(448, 384), vm(896, 256), vm(1280, 256), vm(896, 256), vm(1024, 256),
+            vm(2, 256, 256), vm(2, 256, 256), vm(2, 256, 256), vm(2, 512, 256), vm(384, 512),
+            vm(384, 256), vm(384, 512), vm(2, 192, 256), vm(2, 192, 256), vm(192, 256),
+            vm(192, 256), vm(96, 256), vm(96, 256), vm(2, 96, 256), vm(2, 48, 256),
+            vm(2, 96, 256), vm(2, 48, 256), vm(2, 192, 256), vm(2, 192, 256), vm(2, 96, 512),
+            vm(384, 512),
+            pltpu.SemaphoreType.DMA((3,)),
             pltpu.SemaphoreType.DMA((MESSAGES,)),
             pltpu.SemaphoreType.DMA((MESSAGES,)),
         ],

time: 85.9 us -> 67.5 us (0.79)
  Pallas kernels: 80.5 us -> 62.2 us
    pallas_call x1, Pallas kernels: 80.5 us -> 62.2 us  [fused(): pl.pallas_call(kernel, out_shape=jax.ShapeDtypeStruct(rhs.shape, F32), in...]
where the time goes in v2:
time: 67.5 us; the launch traced here: 67.3 us
  Pallas kernels  62.2 us (92%)
  local copies, waits for them, and re-layouts  5.1 us (8%)
    pallas_call x1, Pallas kernels, fused(): pl.pallas_call(kernel, out_shape=jax.ShapeDtypeStruct(rhs.shape, F32), in...  62.2 us
    unnamed x9, local copies, waits for them, and re-layouts  5.1 us

profile of v2, /device:TPU:0, one launch (start us, length us, event | category | flops | bytes accessed | tf_op | source)
XLA Modules:
  0.0 67.3 jit_solution(9121097627327495215)
XLA Ops:
  0.0 0.0 copy-start
  0.0 1.3 %copy-done = f32[1280,256]{1,0:T(8,128)S(1)} copy-done((f32[1280,256]{1,0:T(8,128)S(1)}, f32[1280,256]{1,0:T(8,128)}, u32[]{:S(2)}) %copy-start) | copy-done | bytes 1310744
  1.3 0.0 copy-start.1
  1.3 1.2 %copy-done.1 = f32[896,256]{1,0:T(8,128)S(1)} copy-done((f32[896,256]{1,0:T(8,128)S(1)}, f32[896,256]{1,0:T(8,128)}, u32[]{:S(2)}) %copy-start.1) | copy-done | bytes 917528
  2.5 0.0 copy-start.2
  2.5 1.1 %copy-done.2 = f32[448,384]{1,0:T(8,128)S(1)} copy-done((f32[448,384]{1,0:T(8,128)S(1)}, f32[448,384]{1,0:T(8,128)}, u32[]{:S(2)}) %copy-start.2) | copy-done | bytes 688152
  3.6 0.0 copy-start.3
  3.6 0.7 copy-done.3
  4.3 62.2 %shard_map.46 = f32[448,384]{1,0:T(8,128)S(1)} custom-call(f32[448,384]{1,0:T(8,128)S(1)} %copy-done.2, f32[896,256]{1,0:T(8,128)S(1)} %copy-done.1, f32[1280,256]{1,0:T(8,128)S(1)} %copy-done, s32[1,3]{1,0:T(1,128)S(1)} %copy-done.3), custom_call_target="tpu_custom_call" | custom-call | tf_op jit(solution)/shard_map/pallas_call | solution.py:337
  66.4 0.8 %copy.6 = f32[448,384]{1,0:T(8,128)} copy(f32[448,384]{1,0:T(8,128)S(1)} %shard_map.46) | data formatting | bytes 1376256
Async XLA Ops:
  0.0 1.3 %copy-start = (f32[1280,256]{1,0:T(8,128)S(1)}, f32[1280,256]{1,0:T(8,128)}, u32[]{:S(2)}) copy-start(f32[1280,256]{1,0:T(8,128)} %lower_hbm.1) | copy-start | bytes 3932164
  1.3 1.2 %copy-start.1 = (f32[896,256]{1,0:T(8,128)S(1)}, f32[896,256]{1,0:T(8,128)}, u32[]{:S(2)}) copy-start(f32[896,256]{1,0:T(8,128)} %dinv_hbm.1) | copy-start | bytes 2752516
  2.5 1.1 %copy-start.2 = (f32[448,384]{1,0:T(8,128)S(1)}, f32[448,384]{1,0:T(8,128)}, u32[]{:S(2)}) copy-start(f32[448,384]{1,0:T(8,128)} %rhs_hbm.1) | copy-start | bytes 2064388
  3.6 0.7 copy-start.3

commit v3 on v2

--- a/solution.py
+++ b/solution.py
@@ -195,6 +195,9 @@
     b12[0] = lower_ref[1024:1280] * pat_ref[0, 2].astype(F32)
     d2[0, 0:128] = dinv_ref[768:896]
     z_b12 = hop(b12.at[0], 0, zl.at[0], 0, 256, Z0)
+    h_d1 = hop(dinv_hbm, 512, xd, 512, 256, xp)
+    h_b12 = hop(b12.at[0], 0, b12.at[1], 0, 256, xp)
+    h_d2 = hop(d2.at[0], 0, d2.at[1], 0, 128, xp)
     z_d2 = [hop(d2.at[0], 0, d2.at[0], 128 * (i + 1), 128, Z) for i, Z in enumerate((Z0, Z1, Z3))]
 
     lane = lax.broadcasted_iota(jnp.int32, (192, 256), 1)
@@ -215,11 +218,9 @@
     c_1 = send(e1.at[0], g1, Z0)
     e2[0] = own_rows(give192, 2) - m02 * dot3(y, lower_ref[512:1024], NN)
     c_2 = send(e2.at[0], g2, Z0)
-    h_d1 = hop(dinv_hbm, 512, xd, 512, 256, xp)
     s_zd1 = share(z_d1, zd.at[0], 0, 256)
     s_zb12 = share(z_b12, zl.at[0], 0, 256)
     q_b.wait_recv()
-    h_b12 = hop(b12.at[0], 0, b12.at[1], 0, 256, xp)
     y = y0[keep192] + dot3(rturned[keep192], xd[0:512], NT)
     y0[keep192] = y
     e1[1] = own_rows(keep192, 1) - m01 * dot3(y, lower_ref[0:512], NN)
@@ -229,9 +230,10 @@
     c_1.wait_recv()
     e1[1] = e1[1] + g1[...]
     t_1 = send(e1.at[1, give96], u1, xp)
-    h_d2 = hop(d2.at[0], 0, d2.at[1], 0, 128, xp)
     s_b12 = share(h_b12, b12.at[1], 0, 256)
     z_xb12 = hop(b12.at[1], 0, zl.at[1], 0, 256, Z0)
+    s_d2 = share(h_d2, d2.at[1], 0, 128)
+    z_xd2 = [hop(d2.at[1], 0, d2.at[1], 128 * (i + 1), 128, Z) for i, Z in enumerate((Z0, Z1, Z3))]
     c_2.wait_recv()
     e2[1] = e2[1] + g2[...]
     t_2 = send(e2.at[1, give96], u2, xp)
@@ -244,8 +246,6 @@
     c1 = [e1[1, keep96], u1[...]]
     s_d1.wait_recv()
     y1[0] = dot3(c1[0], dinv_ref[512:768], NT) + dot3(c1[1], xd[512:768], NT)
-    s_d2 = share(h_d2, d2.at[1], 0, 128)
-    z_xd2 = [hop(d2.at[1], 0, d2.at[1], 128 * (i + 1), 128, Z) for i, Z in enumerate((Z0, Z1, Z3))]
     s_zd1.wait_recv()
     s_xd1.wait_recv()
     y1[1] = dot3(c1[0], zd[0], NT) + dot3(c1[1], zd[1], NT)
@@ -351,7 +351,7 @@
             pltpu.SemaphoreType.DMA((MESSAGES,)),
         ],
         compiler_params=pltpu.CompilerParams(
-            collective_id=0, has_side_effects=True, vmem_limit_bytes=48 * 2**20
+            collective_id=0, has_side_effects=True, vmem_limit_bytes=62 * 2**20
         ),
     )(rhs, dinv, lower, pattern)
 

time: 67.5 us -> 65.2 us (0.966)
  local copies, waits for them, and re-layouts: 5.1 us -> 1.99 us
  Pallas kernels: 62.2 us -> 63.1 us
    unnamed x9 -> x1, local copies, waits for them, and re-layouts: 5.1 us -> 1.99 us
    pallas_call x1, Pallas kernels: 62.2 us -> 63.1 us  [fused(): pl.pallas_call(kernel, out_shape=jax.ShapeDtypeStruct(rhs.shape, F32), in...]
where the time goes in v3:
time: 65.2 us; the launch traced here: 65.1 us
  Pallas kernels  63.1 us (97%)
  local copies, waits for them, and re-layouts  1.99 us (3%)
    pallas_call x1, Pallas kernels, fused(): pl.pallas_call(kernel, out_shape=jax.ShapeDtypeStruct(rhs.shape, F32), in...  63.1 us
    unnamed x1, local copies, waits for them, and re-layouts  1.99 us

profile of v3, /device:TPU:0, one launch (start us, length us, event | category | flops | bytes accessed | tf_op | source)
XLA Modules:
  0.0 65.1 jit_solution(11294227354743819180)
XLA Ops:
  0.0 63.1 %shard_map.46 = f32[448,384]{1,0:T(8,128)} custom-call(f32[448,384]{1,0:T(8,128)} %rhs_hbm.1, f32[896,256]{1,0:T(8,128)} %dinv_hbm.1, f32[1280,256]{1,0:T(8,128)} %lower_hbm.1, s32[1,3]{1,0:T(1,128)} %pat_ref.1), custom_call_target="tpu_custom_call" | custom-call | tf_op jit(solution)/shard_map/pallas_call | solution.py:337
  63.1 2.0 %copy.6 = f32[448,384]{1,0:T(8,128)} copy(f32[448,384]{1,0:T(8,128)} %shard_map.46) | data formatting | bytes 1376256
